TPU v7x, 128 devices: a whole 4x4x4 slice. The times are simulated.
128 devices in a mesh: dp: 16 (over y, z_lo, core), row: 2 (over z_hi), col: 4 (over x).
Axes of the slice: x: 4, y: 4, z: 4 (z_hi: 2, z_lo: 2; z = z_hi * 2 + z_lo), core: 2. Of those that a mesh axis runs over, the one named last changes fastest.
Arguments:
- hidden_in: bfloat16 [19456, 1152], P(('dp', 'row', 'col')), may hold values from -6 to 6
- segments: int32 [19456], P('dp'), may hold values from 0 to 1, as said below
- positions: int32 [19456], P('dp'), may hold values from 0 to 4095, as said below
- out_grad: bfloat16 [19456, 1152], P(('dp', 'row', 'col')), may hold values from -6 to 6
- w_query: bfloat16 [1152, 1024], P('row', ('col', 'dp')), may hold values from -0.1875 to 0.1875
- w_key: bfloat16 [1152, 256], P('row', 'dp'), may hold values from -0.1875 to 0.1875
- w_value: bfloat16 [1152, 256], P('row', 'dp'), may hold values from -0.1875 to 0.1875
- w_out: bfloat16 [1024, 1152], P('col', ('row', 'dp')), may hold values from -0.1875 to 0.1875
- w_gate: bfloat16 [1152, 6912], P('row', ('col', 'dp')), may hold values from -0.1875 to 0.1875
- w_up: bfloat16 [1152, 6912], P('row', ('col', 'dp')), may hold values from -0.1875 to 0.1875
- w_down: bfloat16 [6912, 1152], P('col', ('row', 'dp')), may hold values from -0.078125 to 0.078125
- norm_gains: bfloat16 [4, 1152], P(None, ('row', 'col', 'dp')), may hold values from 0.25 to 1.75
- head_gains: bfloat16 [2, 256], P(None, 'dp'), may hold values from 0.25 to 1.75
Outputs:
- result: bfloat16 [19456, 1152], P(('dp', 'row', 'col'))
- input_grad: bfloat16 [19456, 1152], P(('dp', 'row', 'col'))
- grad_query: float32 [1152, 1024], P('row', ('col', 'dp'))
- grad_key: float32 [1152, 256], P('row', 'dp')
- grad_value: float32 [1152, 256], P('row', 'dp')
- grad_out: float32 [1024, 1152], P('col', ('row', 'dp'))
- grad_gate: float32 [1152, 6912], P('row', ('col', 'dp'))
- grad_up: float32 [1152, 6912], P('row', ('col', 'dp'))
- grad_down: float32 [6912, 1152], P('col', ('row', 'dp'))
- grad_norm_gains: float32 [4, 1152], P(None, ('row', 'col', 'dp'))
- grad_head_gains: float32 [2, 256], P(None, 'dp')
Inputs may be any that keep to these rules, and one draw needn't show every extreme that they name: `segments`: in each sequence of 1216 tokens, segment 0 comes first and segment 1 follows; the shorter document has 202 to 303 tokens and lies at either end. Within a document positions rise by one from a start drawn for that document; every draw holds position 0 and position 4095.
All inputs are finite; a program needn't handle non-finite values.
Results may differ from a plain program's by a relative error of at most 0.035.
Values may be sent and summed in bfloat16 or wider, within the bound.
No kernel may reach another device: no remote copies, remote signals or barrier semaphores. Data moves between devices by JAX's collectives and lax.ppermute only.
A program may use at most 128 MiB of HBM per device.

v0:
```python
import math

import jax
import jax.numpy as jnp
from jax import lax
from jax.sharding import PartitionSpec as P

D = 1152
HD = 256
LEN = 1216


EPSILON = 1e-06
ROPE_BASE = 1000000.0
MASKED = -1e30


def rotary_tables(places, head_width):
    frequencies = jnp.exp(
        jnp.arange(head_width // 2, dtype=jnp.float32) * (-2.0 * math.log(ROPE_BASE) / head_width)
    )
    angles = places.astype(jnp.float32)[:, None] * frequencies[None, :]
    return (jnp.cos(angles), jnp.sin(angles))


def rotate(values, cosine, sine_part):
    midpoint = values.shape[-1] // 2
    front_half = values[..., :midpoint]
    back_half = values[..., midpoint:]
    cos_rows = cosine[:, None, :]
    sin_rows = sine_part[:, None, :]
    return jnp.concatenate(
        [
            front_half * cos_rows - back_half * sin_rows,
            back_half * cos_rows + front_half * sin_rows,
        ],
        axis=-1,
    )


def norm_rotate(raw_values, gain_row, cosine, sine_part):
    inverse = lax.rsqrt(jnp.mean(raw_values * raw_values, axis=-1, keepdims=True) + EPSILON)
    return rotate(raw_values * inverse * gain_row, cosine, sine_part)


def width_total(values):
    return lax.psum(values, ("row", "col"))


def inverse_rms(values):
    return lax.rsqrt(width_total(jnp.sum(values * values, axis=1)) / D + EPSILON)[:, None]


def norm_backward(upstream, source, inverse, gain_row):
    weighted = upstream * gain_row
    inner = width_total(jnp.sum(weighted * source, axis=1))[:, None] / D
    source_grad = inverse * weighted - source * (inverse * inverse * inverse) * inner
    gain_grad = jnp.sum(upstream * source * inverse, axis=0)
    return (source_grad, gain_grad)


def spread_width(values):
    return lax.all_gather(values, "col", axis=1, tiled=True)


def reduce_width(values):
    return lax.psum_scatter(
        values.astype(jnp.bfloat16), "col", scatter_dimension=1, tiled=True
    ).astype(jnp.float32)


def query_total(values):
    return lax.psum_scatter(values, "row", scatter_dimension=0, tiled=True)


def query_spread(values):
    return lax.all_gather(values, "row", axis=0, tiled=True)


def on_device(
    hidden_in,
    segments,
    positions,
    out_grad,
    w_query,
    w_key,
    w_value,
    w_out,
    w_gate,
    w_up,
    w_down,
    norm_gains,
    head_gains,
):
    stream_low, upstream_low = (
        lax.all_to_all(hidden_in, ("row", "col"), split_axis=1, concat_axis=0, tiled=True),
        lax.all_to_all(out_grad, ("row", "col"), split_axis=1, concat_axis=0, tiled=True),
    )
    gathered = (
        lax.all_gather(w_query, "dp", axis=1, tiled=True),
        lax.all_gather(w_key, "dp", axis=1, tiled=True),
        lax.all_gather(w_value, "dp", axis=1, tiled=True),
        lax.all_gather(w_out, "dp", axis=1, tiled=True),
        lax.all_gather(w_gate, "dp", axis=1, tiled=True),
        lax.all_gather(w_up, "dp", axis=1, tiled=True),
        lax.all_gather(w_down, "dp", axis=1, tiled=True),
        lax.all_gather(norm_gains, "dp", axis=1, tiled=True),
        lax.all_gather(head_gains, "dp", axis=1, tiled=True),
    )
    (
        query_weight,
        key_weight,
        value_weight,
        out_weight,
        gate_weight,
        up_weight,
        down_weight,
        gains_low,
        head_low,
    ) = gathered
    gain_rows = gains_low.astype(jnp.float32)
    head_gain = head_low.astype(jnp.float32)
    col_count = lax.axis_size("col")
    row_count = lax.axis_size("row")
    token_count = stream_low.shape[0]
    score_scale = HD ** (-0.5)
    stream = stream_low.astype(jnp.float32)
    scale_one = inverse_rms(stream)
    wide_one = spread_width((stream * scale_one * gain_rows[0]).astype(jnp.bfloat16))
    query_raw = query_total(jnp.dot(wide_one, query_weight, preferred_element_type=jnp.float32))
    key_raw, value_raw = lax.psum(
        (
            jnp.dot(wide_one, key_weight, preferred_element_type=jnp.float32),
            jnp.dot(wide_one, value_weight, preferred_element_type=jnp.float32),
        ),
        "row",
    )
    query_rows = query_raw.shape[0]
    head_count = query_raw.shape[1] // HD
    row_start = lax.axis_index("row") * query_rows
    query_places = lax.dynamic_slice_in_dim(positions, row_start, query_rows)
    query_segments = lax.dynamic_slice_in_dim(segments, row_start, query_rows)
    query_cos, query_sin = rotary_tables(query_places, HD)
    key_cos, key_sin = rotary_tables(positions, HD)
    query_norm, query_back = jax.vjp(
        lambda raw_part, gain_part: norm_rotate(raw_part, gain_part, query_cos, query_sin),
        query_raw.reshape(query_rows, head_count, HD),
        head_gain[0],
    )
    key_norm, key_back = jax.vjp(
        lambda raw_part, gain_part: norm_rotate(raw_part, gain_part, key_cos, key_sin),
        key_raw.reshape(token_count, 1, HD),
        head_gain[1],
    )
    query_rot = query_norm.astype(jnp.bfloat16)
    key_rot = key_norm.reshape(token_count, HD).astype(jnp.bfloat16)
    value_low = value_raw.astype(jnp.bfloat16)
    block_rows = LEN // row_count
    block_count = query_rows // block_rows

    def block_scores(block_index):
        offset = block_index * block_rows
        token_start = row_start + offset
        key_start = token_start // LEN * LEN
        query_order = token_start + jnp.arange(block_rows, dtype=jnp.int32)
        key_order = key_start + jnp.arange(LEN, dtype=jnp.int32)
        allowed = (query_segments[:, None] == segments[None, :]) & (
            query_order[:, None] >= key_order[None, :]
        )
        scores = (
            jnp.einsum("qhd,kd->hqk", query_rot, key_rot, preferred_element_type=jnp.float32)
            * score_scale
        )
        scores = jnp.where(allowed[None], scores, MASKED)
        return (scores, query_rot, key_rot, value_low, key_start)

    def attend_block(block_index):
        scores, query_block, key_block, value_block, key_start = block_scores(block_index)
        highest = jnp.max(scores, axis=-1, keepdims=True)
        exponent = jnp.exp(scores - highest)
        totals = jnp.sum(exponent, axis=-1, keepdims=True)
        probs_low = (exponent / totals).astype(jnp.bfloat16)
        context = jnp.einsum(
            "hqk,kd->qhd", probs_low, value_block, preferred_element_type=jnp.float32
        )
        return (context.astype(jnp.bfloat16), highest, totals)

    context_blocks, highest_kept, totals_kept = lax.map(
        attend_block, jnp.arange(block_count, dtype=jnp.int32)
    )
    context_low = context_blocks.reshape(query_rows, head_count * HD)
    context_all = query_spread(context_low)
    attn_raw = reduce_width(jnp.dot(context_all, out_weight, preferred_element_type=jnp.float32))
    scale_two = inverse_rms(attn_raw)
    middle = stream + attn_raw * scale_two * gain_rows[1]
    scale_three = inverse_rms(middle)
    normed_two_low = (middle * scale_three * gain_rows[2]).astype(jnp.bfloat16)
    upstream = upstream_low.astype(jnp.float32)
    wide_two = spread_width(normed_two_low)
    gate_raw, up_raw = (
        lax.psum_scatter(
            jnp.dot(wide_two, gate_weight, preferred_element_type=jnp.float32).astype(jnp.bfloat16),
            "row",
            scatter_dimension=1,
            tiled=True,
        ).astype(jnp.float32),
        lax.psum_scatter(
            jnp.dot(wide_two, up_weight, preferred_element_type=jnp.float32).astype(jnp.bfloat16),
            "row",
            scatter_dimension=1,
            tiled=True,
        ).astype(jnp.float32),
    )
    activated, gelu_back = jax.vjp(
        lambda gate_in, up_in: jax.nn.gelu(gate_in, approximate=True) * up_in, gate_raw, up_raw
    )
    hidden_all = lax.all_gather(activated.astype(jnp.bfloat16), "row", axis=1, tiled=True)
    down_raw = reduce_width(jnp.dot(hidden_all, down_weight, preferred_element_type=jnp.float32))
    scale_four = inverse_rms(down_raw)
    result = middle + down_raw * scale_four * gain_rows[3]
    down_grad, gain_four = norm_backward(upstream, down_raw, scale_four, gain_rows[3])
    down_wide = spread_width(down_grad.astype(jnp.bfloat16))
    grad_down_w = jnp.einsum("tf,td->fd", hidden_all, down_wide, preferred_element_type=jnp.float32)
    hidden_grad = lax.psum_scatter(
        jnp.einsum("td,fd->tf", down_wide, down_weight, preferred_element_type=jnp.float32).astype(
            jnp.bfloat16
        ),
        "row",
        scatter_dimension=1,
        tiled=True,
    ).astype(jnp.float32)
    gate_grad, up_grad = gelu_back(hidden_grad)
    gate_wide, up_wide = (
        lax.all_gather(gate_grad.astype(jnp.bfloat16), "row", axis=1, tiled=True),
        lax.all_gather(up_grad.astype(jnp.bfloat16), "row", axis=1, tiled=True),
    )
    grad_gate_w = jnp.einsum("td,tf->df", wide_two, gate_wide, preferred_element_type=jnp.float32)
    grad_up_w = jnp.einsum("td,tf->df", wide_two, up_wide, preferred_element_type=jnp.float32)
    normed_two_grad = reduce_width(
        jnp.einsum("tf,df->td", gate_wide, gate_weight, preferred_element_type=jnp.float32)
        + jnp.einsum("tf,df->td", up_wide, up_weight, preferred_element_type=jnp.float32)
    )
    middle_part, gain_three = norm_backward(normed_two_grad, middle, scale_three, gain_rows[2])
    middle_grad = upstream + middle_part
    attn_grad, gain_two = norm_backward(middle_grad, attn_raw, scale_two, gain_rows[1])
    attn_wide = spread_width(attn_grad.astype(jnp.bfloat16))
    grad_out_w = jnp.einsum("tq,td->qd", context_all, attn_wide, preferred_element_type=jnp.float32)
    context_grad = query_total(
        jnp.einsum("td,qd->tq", attn_wide, out_weight, preferred_element_type=jnp.float32)
    ).astype(jnp.bfloat16)
    context_heads = context_grad.reshape(query_rows, head_count, HD)

    def attend_grad(running, block_index):
        key_total, value_total = running
        scores, query_block, key_block, value_block, key_start = block_scores(block_index)
        probs = jnp.exp(scores - highest_kept[block_index]) / totals_kept[block_index]
        probs_low = probs.astype(jnp.bfloat16)
        prob_grad = jnp.einsum(
            "qhd,kd->hqk", context_heads, value_block, preferred_element_type=jnp.float32
        )
        centre = jnp.sum(probs * prob_grad, axis=-1, keepdims=True)
        score_low = (probs * (prob_grad - centre)).astype(jnp.bfloat16)
        query_part = (
            jnp.einsum("hqk,kd->qhd", score_low, key_block, preferred_element_type=jnp.float32)
            * score_scale
        )
        key_part = (
            jnp.einsum("hqk,qhd->kd", score_low, query_block, preferred_element_type=jnp.float32)
            * score_scale
        )
        value_part = jnp.einsum(
            "hqk,qhd->kd", probs_low, context_heads, preferred_element_type=jnp.float32
        )
        key_total = key_total + key_part
        value_total = value_total + value_part
        return ((key_total, value_total), query_part)

    zero_rows = jnp.zeros((token_count, HD), jnp.float32)
    (key_partial, value_partial), query_blocks = lax.scan(
        attend_grad, (zero_rows, zero_rows), jnp.arange(block_count, dtype=jnp.int32)
    )
    query_raw_grad, query_gain_part = query_back(query_blocks.reshape(query_rows, head_count, HD))
    key_summed, value_summed, query_gain_grad = (
        lax.psum(key_partial.astype(jnp.bfloat16), ("row", "col")).astype(jnp.float32),
        lax.psum(value_partial.astype(jnp.bfloat16), ("row", "col")).astype(jnp.float32),
        lax.psum(query_gain_part.astype(jnp.bfloat16), ("row", "col")).astype(jnp.float32),
    )
    key_raw_grad, key_gain_grad = key_back(key_summed.reshape(token_count, 1, HD))
    query_wide = query_spread(
        query_raw_grad.reshape(query_rows, head_count * HD).astype(jnp.bfloat16)
    )
    key_grad_low = key_raw_grad.reshape(token_count, HD).astype(jnp.bfloat16)
    value_grad_low = value_summed.astype(jnp.bfloat16)
    grad_query_w = jnp.einsum("td,tq->dq", wide_one, query_wide, preferred_element_type=jnp.float32)
    grad_key_w = jnp.einsum("td,tk->dk", wide_one, key_grad_low, preferred_element_type=jnp.float32)
    grad_value_w = jnp.einsum(
        "td,tk->dk", wide_one, value_grad_low, preferred_element_type=jnp.float32
    )
    shared_part = (
        jnp.einsum("tk,dk->td", key_grad_low, key_weight, preferred_element_type=jnp.float32)
        + jnp.einsum("tk,dk->td", value_grad_low, value_weight, preferred_element_type=jnp.float32)
    ) * (1.0 / col_count)
    normed_one_grad = reduce_width(
        jnp.einsum("tq,dq->td", query_wide, query_weight, preferred_element_type=jnp.float32)
        + shared_part
    )
    stream_part, gain_one = norm_backward(normed_one_grad, stream, scale_one, gain_rows[0])
    input_grad = (middle_grad + stream_part).astype(jnp.bfloat16)
    gains_grad = jnp.stack([gain_one, gain_two, gain_three, gain_four])
    head_grad = jnp.stack([query_gain_grad, key_gain_grad])
    summed = (
        lax.psum_scatter(
            grad_query_w.astype(jnp.bfloat16), "dp", scatter_dimension=1, tiled=True
        ).astype(jnp.float32),
        lax.psum_scatter(
            grad_key_w.astype(jnp.bfloat16), "dp", scatter_dimension=1, tiled=True
        ).astype(jnp.float32),
        lax.psum_scatter(
            grad_value_w.astype(jnp.bfloat16), "dp", scatter_dimension=1, tiled=True
        ).astype(jnp.float32),
        lax.psum_scatter(
            grad_out_w.astype(jnp.bfloat16), "dp", scatter_dimension=1, tiled=True
        ).astype(jnp.float32),
        lax.psum_scatter(
            grad_gate_w.astype(jnp.bfloat16), "dp", scatter_dimension=1, tiled=True
        ).astype(jnp.float32),
        lax.psum_scatter(
            grad_up_w.astype(jnp.bfloat16), "dp", scatter_dimension=1, tiled=True
        ).astype(jnp.float32),
        lax.psum_scatter(
            grad_down_w.astype(jnp.bfloat16), "dp", scatter_dimension=1, tiled=True
        ).astype(jnp.float32),
        lax.psum_scatter(
            gains_grad.astype(jnp.bfloat16), "dp", scatter_dimension=1, tiled=True
        ).astype(jnp.float32),
        lax.psum_scatter(
            head_grad.astype(jnp.bfloat16), "dp", scatter_dimension=1, tiled=True
        ).astype(jnp.float32),
    )
    (
        query_shard,
        key_shard,
        value_shard,
        out_shard,
        gate_shard,
        up_shard,
        down_shard,
        gains_shard,
        head_shard,
    ) = summed
    result_rows, grad_rows = (
        lax.all_to_all(
            result.astype(jnp.bfloat16), ("row", "col"), split_axis=0, concat_axis=1, tiled=True
        ),
        lax.all_to_all(input_grad, ("row", "col"), split_axis=0, concat_axis=1, tiled=True),
    )
    return (
        result_rows,
        grad_rows,
        query_shard,
        key_shard,
        value_shard,
        out_shard,
        gate_shard,
        up_shard,
        down_shard,
        gains_shard,
        head_shard,
    )


def solution(mesh):
    return jax.shard_map(
        on_device,
        mesh=mesh,
        in_specs=(
            P(("dp", "row", "col"), None),
            P("dp"),
            P("dp"),
            P(("dp", "row", "col"), None),
            P("row", ("col", "dp")),
            P("row", "dp"),
            P("row", "dp"),
            P("col", ("row", "dp")),
            P("row", ("col", "dp")),
            P("row", ("col", "dp")),
            P("col", ("row", "dp")),
            P(None, ("row", "col", "dp")),
            P(None, "dp"),
        ),
        out_specs=(
            P(("dp", "row", "col"), None),
            P(("dp", "row", "col"), None),
            P("row", ("col", "dp")),
            P("row", "dp"),
            P("row", "dp"),
            P("col", ("row", "dp")),
            P("row", ("col", "dp")),
            P("row", ("col", "dp")),
            P("col", ("row", "dp")),
            P(None, ("row", "col", "dp")),
            P(None, "dp"),
        ),
        check_vma=False,
    )
```

profile of v0, /device:TPU:1, one launch (start us, length us, event | category | flops | bytes accessed | tf_op | source)
XLA Modules:
  0.0 1540.9 jit_solution(4082473066676314883)
XLA Ops:
  18.3 20.4 %all-gather.2 = bf16[16,9,4]{1,2,0:T(4,128)(2,1)S(1)} all-gather(bf16[1,9,4]{1,2,0:T(4,128)(2,1)} %bitcast.255), channel_id=1, replica_groups=mesh['dp'=16,'row'=2,'col'=4] {'dp'}, dimensions={0}, use_global_device_ids=true | all-gather | bytes 1224 | tf_op jit(solution)/shard_map/all_gather | solution.py:107
  39.8 21.8 %psum.91 = f32[1216]{0:T(1024)S(1)} all-reduce(f32[1216]{0:T(1024)S(1)} %reduce_sum.204), channel_id=1, replica_groups=mesh['dp'=16,'row'=2,'col'=4] {'row','col'}, use_global_device_ids=true, to_apply=%region_1.0 | all-reduce | flops 1216 | bytes 9728 | tf_op jit(solution)/shard_map/psum | solution.py:47
  64.5 19.6 %all-gather.3 = bf16[16,16,2]{1,2,0:T(2,128)(2,1)S(1)} all-gather(bf16[1,16,2]{1,2,0:T(2,128)(2,1)S(1)} %bitcast.256), channel_id=1, replica_groups=mesh['dp'=16,'row'=2,'col'=4] {'dp'}, dimensions={0}, use_global_device_ids=true | all-gather | bytes 1088 | tf_op jit(solution)/shard_map/all_gather | solution.py:108
  164.6 40.9 %all-reduce.22 = bf16[1216,256]{1,0:T(8,128)(2,1)S(1)} all-reduce(f32[1216,256]{1,0:T(8,128)S(1)} %fusion.139), channel_id=1, replica_groups=mesh['dp'=16,'row'=2,'col'=4] {'row'}, use_global_device_ids=true, to_apply=%region_2.0 | all-reduce | flops 311296 | bytes 1867776 | tf_op jit(solution)/shard_map/psum | solution.py:131
  236.4 25.2 %reduce-scatter.33.cloned.1.call-done = bf16[1216,144]{0,1:T(8,128)(2,1)} async-done(((bf16[1216,576]{0,1:T(8,128)(2,1)}), bf16[1216,144]{0,1:T(8,128)(2,1)}) %reduce-scatter.33.cloned.1.call-update) | async-done | bytes 350224 | tf_op jit(solution)/shard_map/reduce_scatter | solution.py:67
  262.6 20.1 %psum.94 = f32[1216]{0:T(1024)S(1)} all-reduce(f32[1216]{0:T(1024)S(1)} %fusion.67), channel_id=1, replica_groups=mesh['dp'=16,'row'=2,'col'=4] {'row','col'}, use_global_device_ids=true, to_apply=%region_11.12 | all-reduce | flops 1216 | bytes 9728 | tf_op jit(solution)/shard_map/psum | solution.py:47
  306.6 26.3 %all-gather.24.cloned.1.call-done = bf16[1216,576]{0,1:T(8,128)(2,1)} async-done(((bf16[1216,144]{0,1:T(8,128)(2,1)}), bf16[1216,576]{0,1:T(8,128)(2,1)}) %all-gather.24.cloned.1.call-update) | async-done | bytes 1400848 | tf_op jit(solution)/shard_map/all_gather | solution.py:63
  348.0 64.2 %all-gather.30.cloned.1.call-done = bf16[16,108,576]{2,1,0:T(8,128)(2,1)} async-done(((bf16[1,108,576]{2,1,0:T(8,128)(2,1)}), bf16[16,108,576]{2,1,0:T(8,128)(2,1)}) %all-gather.30.cloned.1.call-update) | async-done | bytes 1990672 | tf_op jit(solution)/shard_map/all_gather | solution.py:104
  433.8 60.9 %reduce-scatter.49.cloned.1.call-done = bf16[864,1216]{1,0:T(8,128)(2,1)} async-done(((bf16[1728,1216]{1,0:T(8,128)(2,1)}), bf16[864,1216]{1,0:T(8,128)(2,1)}) %reduce-scatter.49.cloned.1.call-update) | async-done | bytes 2101264
  514.5 61.5 %all-gather.34.cloned.1.call-done = bf16[2,864,1216]{1,2,0:T(8,128)(2,1)} async-done(((bf16[1,864,1216]{1,2,0:T(8,128)(2,1)}), bf16[2,864,1216]{1,2,0:T(8,128)(2,1)}) %all-gather.34.cloned.1.call-update) | async-done | bytes 4202512 | tf_op jit(solution)/shard_map/all_gather | solution.py:217
  658.4 31.3 %all-gather.26.cloned.1.call-done = bf16[1216,576]{0,1:T(8,128)(2,1)} async-done(((bf16[1216,144]{0,1:T(8,128)(2,1)}), bf16[1216,576]{0,1:T(8,128)(2,1)}) %all-gather.26.cloned.1.call-update) | async-done | bytes 1400848 | tf_op jit(solution)/shard_map/all_gather | solution.py:63
  704.6 61.4 %reduce-scatter.53.cloned.1.call-done = bf16[864,1216]{1,0:T(8,128)(2,1)} async-done(((bf16[1728,1216]{1,0:T(8,128)(2,1)}), bf16[864,1216]{1,0:T(8,128)(2,1)}) %reduce-scatter.53.cloned.1.call-update) | async-done | bytes 2101264
  778.0 61.2 %all-gather.38.cloned.1.call-done = bf16[2,864,1216]{1,2,0:T(8,128)(2,1)} async-done(((bf16[1,864,1216]{1,2,0:T(8,128)(2,1)}), bf16[2,864,1216]{1,2,0:T(8,128)(2,1)}) %all-gather.38.cloned.1.call-update) | async-done | bytes 4202512 | tf_op jit(solution)/shard_map/all_gather | solution.py:234
  853.2 49.7 %all-gather.40.cloned.1.call-done = bf16[2,864,1216]{1,2,0:T(8,128)(2,1)} async-done(((bf16[1,864,1216]{1,2,0:T(8,128)(2,1)}), bf16[2,864,1216]{1,2,0:T(8,128)(2,1)}) %all-gather.40.cloned.1.call-update) | async-done | bytes 4202512 | tf_op jit(solution)/shard_map/all_gather | solution.py:235
  918.0 22.9 %reduce-scatter.37.cloned.1.call-done = bf16[1216,144]{0,1:T(8,128)(2,1)} async-done(((bf16[1216,576]{0,1:T(8,128)(2,1)}), bf16[1216,144]{0,1:T(8,128)(2,1)}) %reduce-scatter.37.cloned.1.call-update) | async-done | bytes 350224 | tf_op jit(solution)/shard_map/reduce_scatter | solution.py:67
  942.7 20.1 %psum.98 = f32[1216]{0:T(1024)S(1)} all-reduce(f32[1216]{0:T(1024)S(1)} %get-tuple-element.76), channel_id=1, replica_groups=mesh['dp'=16,'row'=2,'col'=4] {'row','col'}, use_global_device_ids=true, to_apply=%region_24.25 | all-reduce | flops 1216 | bytes 9728 | tf_op jit(solution)/shard_map/psum | solution.py:47
  982.5 31.4 %all-gather.28.cloned.1.call-done = bf16[1216,576]{0,1:T(8,128)(2,1)} async-done(((bf16[1216,144]{0,1:T(8,128)(2,1)}), bf16[1216,576]{0,1:T(8,128)(2,1)}) %all-gather.28.cloned.1.call-update) | async-done | bytes 1400848 | tf_op jit(solution)/shard_map/all_gather | solution.py:63
  1017.2 27.3 %reduce-scatter.39.cloned.1.call-done = f32[608,256]{1,0:T(8,128)} async-done(((f32[1216,256]{1,0:T(8,128)}), f32[608,256]{1,0:T(8,128)}) %reduce-scatter.39.cloned.1.call-update) | async-done | bytes 622608 | tf_op jit(solution)/shard_map/reduce_scatter | solution.py:73
  1071.4 63.5 %all-reduce.21.cloned.1.call-done = (bf16[1216,1,256]{2,0,1:T(8,128)(2,1)}, bf16[1216,256]{1,0:T(8,128)(2,1)}) async-done(((bf16[1216,1,256]{2,0,1:T(8,128)(2,1)}, bf16[1216,256]{1,0:T(8,128)(2,1)}), (bf16[1216,1,256]{2,0,1:T(8,128)(2,1)}, bf16[1216,256]{1,0:T(8,128)(2,1)})) %all-reduce.21.cloned.1.call-update) | async-done | bytes 1245200 | tf_op jit(solution)/shard_map/psum | solution.py:284
  1175.9 91.7 %fusion.132 = (bf16[256,40]{0,1:T(8,128)(2,1)}, bf16[576,112]{0,1:T(8,128)(2,1)}, bf16[576,112]{0,1:T(8,128)(2,1)}, bf16[1728,40]{0,1:T(8,128)(2,1)}) fusion(bf16[256,576]{0,1:T(8,128)(2,1)} %convolution_convert_fusion.12, bf16[576,1728]{0,1:T(8,128)(2,1)} %convolution_convert_fusion.4, bf16[576,1728]{0,1:T(8,128)(2,1)} %convolution_convert_fusion.3, ...), kind=kCustom, calls=%all-reduce-scatter.4 | all-reduce-scatter fusion | flops 3334146 | bytes 6684160
  1297.6 21.3 %psum.103 = bf16[1,256]{1,0:T(2,128)(2,1)S(1)} all-reduce(bf16[1,256]{1,0:T(2,128)(2,1)S(1)} %stack.37), channel_id=1, replica_groups=mesh['dp'=16,'row'=2,'col'=4] {'row','col'}, use_global_device_ids=true, to_apply=%region_49.50 | all-reduce | flops 256 | bytes 1024 | tf_op jit(solution)/shard_map/psum | solution.py:286
  1377.3 60.4 %reduce-scatter.47.cloned.1.call-done = bf16[576,16]{0,1:T(8,128)(2,1)} async-done(((bf16[576,256]{0,1:T(8,128)(2,1)}), bf16[576,16]{0,1:T(8,128)(2,1)}) %reduce-scatter.47.cloned.1.call-update) | async-done | bytes 18448 | tf_op jit(solution)/shard_map/reduce_scatter | solution.py:318
  1439.1 60.1 %reduce-scatter.45.cloned.1.call-done = bf16[576,16]{0,1:T(8,128)(2,1)} async-done(((bf16[576,256]{0,1:T(8,128)(2,1)}), bf16[576,16]{0,1:T(8,128)(2,1)}) %reduce-scatter.45.cloned.1.call-update) | async-done | bytes 18448 | tf_op jit(solution)/shard_map/reduce_scatter | solution.py:315
  1500.5 30.9 %all-reduce.8 = bf16[4,144]{1,0:T(4,128)(2,1)S(1)} all-reduce(bf16[4,144]{1,0:T(4,128)(2,1)S(1)} %pad_maximum_fusion.3), channel_id=20, replica_groups=mesh['dp'=16,'row'=2,'col'=4] {'dp'}, use_global_device_ids=true, to_apply=%region_47.48.clone | all-reduce | flops 576 | bytes 2304
  (389 shorter events, 527.9 us)
Async XLA Ops:
  18.2 102.0 %all-gather.22.cloned.1.call-start = ((), (), s32[]{:S(2)}) async-start(), calls=%async_computation.17 | async-start | bytes 1843200 | tf_op jit(solution)/shard_map/all_gather | solution.py:63
  64.5 141.1 %all-reduce.19.cloned.1.call-start = ((), (), s32[]{:S(2)}) async-start(), calls=%async_computation.18 | async-start | bytes 2490368 | tf_op jit(solution)/shard_map/psum | solution.py:131
  123.6 92.0 %reduce-scatter.31.cloned.1.call-start = ((), (), s32[]{:S(2)}) async-start(), calls=%async_computation.19 | async-start | bytes 1867776 | tf_op jit(solution)/shard_map/reduce_scatter | solution.py:73
  164.6 96.9 %reduce-scatter.33.cloned.1.call-start = ((), (), s32[]{:S(2)}) async-start(), calls=%async_computation.20 | async-start | bytes 1843200 | tf_op jit(solution)/shard_map/reduce_scatter | solution.py:67
  236.1 96.9 %all-gather.24.cloned.1.call-start = ((), (), s32[]{:S(2)}) async-start(), calls=%async_computation.21 | async-start | bytes 1843200 | tf_op jit(solution)/shard_map/all_gather | solution.py:63
  301.8 110.4 %all-gather.30.cloned.1.call-start = ((), (), s32[]{:S(2)}) async-start(), calls=%async_computation.31 | async-start | bytes 2437120 | tf_op jit(solution)/shard_map/all_gather | solution.py:104
  302.3 128.4 %reduce-scatter.51.cloned.1.call-start = ((), (), s32[]{:S(2)}) async-start(), calls=%async_computation.38 | async-start | bytes 6635520
  347.9 146.8 %reduce-scatter.49.cloned.1.call-start = ((), (), s32[]{:S(2)}) async-start(), calls=%async_computation.37 | async-start | bytes 6635520
  430.6 145.4 %all-gather.34.cloned.1.call-start = ((), (), s32[]{:S(2)}) async-start(), calls=%async_computation.33 | async-start | bytes 6537216 | tf_op jit(solution)/shard_map/all_gather | solution.py:217
  503.8 113.9 %reduce-scatter.35.cloned.1.call-start = ((), (), s32[]{:S(2)}) async-start(), calls=%async_computation.22 | async-start | bytes 1843200 | tf_op jit(solution)/shard_map/reduce_scatter | solution.py:67
  590.1 99.6 %all-gather.26.cloned.1.call-start = ((), (), s32[]{:S(2)}) async-start(), calls=%async_computation.23 | async-start | bytes 1843200 | tf_op jit(solution)/shard_map/all_gather | solution.py:63
  658.3 107.6 %reduce-scatter.53.cloned.1.call-start = ((), (), s32[]{:S(2)}) async-start(), calls=%async_computation.39 | async-start | bytes 6635520
  704.5 134.7 %all-gather.38.cloned.1.call-start = ((), (), s32[]{:S(2)}) async-start(), calls=%async_computation.35 | async-start | bytes 6537216 | tf_op jit(solution)/shard_map/all_gather | solution.py:234
  777.0 125.9 %all-gather.40.cloned.1.call-start = ((), (), s32[]{:S(2)}) async-start(), calls=%async_computation.36 | async-start | bytes 6537216 | tf_op jit(solution)/shard_map/all_gather | solution.py:235
  777.8 163.2 %reduce-scatter.37.cloned.1.call-start = ((), (), s32[]{:S(2)}) async-start(), calls=%async_computation.24 | async-start | bytes 1843200 | tf_op jit(solution)/shard_map/reduce_scatter | solution.py:67
  917.9 96.0 %all-gather.28.cloned.1.call-start = ((), (), s32[]{:S(2)}) async-start(), calls=%async_computation.25 | async-start | bytes 1843200 | tf_op jit(solution)/shard_map/all_gather | solution.py:63
  1017.2 117.7 %all-reduce.21.cloned.1.call-start = ((), (), s32[]{:S(2)}) async-start(), calls=%async_computation.41 | async-start | bytes 2490368 | tf_op jit(solution)/shard_map/psum | solution.py:284
  1052.5 281.9 %reduce-scatter.41.cloned.1.call-start = ((), (), s32[]{:S(2)}) async-start(), calls=%async_computation.27 | async-start | bytes 1843200 | tf_op jit(solution)/shard_map/reduce_scatter | solution.py:67
  1166.6 112.3 %all-to-all-start.1 = ((bf16[8,152,144]{1,2,0:T(8,128)(2,1)}), bf16[8,152,144]{1,2,0:T(8,128)(2,1)S(1)}, u32[]{:S(2)}, u32[]{:S(2)}) async-start(bf16[8,152,144]{1,2,0:T(8,128)(2,1)} %copy.66), calls=%async_computation.4 | async-start | bytes 1179648 | tf_op jit(solution)/shard_map/all_to_all | solution.py:352
  1170.2 188.5 %reduce-scatter.43.cloned.1.call-start = ((), (), s32[]{:S(2)}) async-start(), calls=%async_computation.28 | async-start | bytes 348160 | tf_op jit(solution)/shard_map/reduce_scatter | solution.py:312
  1173.1 202.9 %reduce-scatter.55.cloned.1.call-start = ((), (), s32[]{:S(2)}) async-start(), calls=%async_computation.40 | async-start | bytes 69632
  1320.4 117.4 %reduce-scatter.47.cloned.1.call-start = ((), (), s32[]{:S(2)}) async-start(), calls=%async_computation.30 | async-start | bytes 348160 | tf_op jit(solution)/shard_map/reduce_scatter | solution.py:318
  1323.0 176.1 %reduce-scatter.45.cloned.1.call-start = ((), (), s32[]{:S(2)}) async-start(), calls=%async_computation.29 | async-start | bytes 348160 | tf_op jit(solution)/shard_map/reduce_scatter | solution.py:315
  1354.4 177.7 %all-to-all-start.3 = ((bf16[8,152,144]{1,2,0:T(8,128)(2,1)}), bf16[8,152,144]{1,2,0:T(8,128)(2,1)S(1)}, u32[]{:S(2)}, u32[]{:S(2)}) async-start(bf16[8,152,144]{1,2,0:T(8,128)(2,1)} %copy.72), calls=%async_computation.9 | async-start | bytes 1179648 | tf_op jit(solution)/shard_map/all_to_all | solution.py:355
  (90 other events, 2492.7 us)
Sparse Core Ops, SparseCore 0:
  64.6 22.2 all-gather.21
  123.7 51.3 all-reduce.18
  177.6 37.8 reduce-scatter.30
  235.6 25.8 reduce-scatter.32
  348.0 63.3 reduce-scatter.50
  430.0 64.6 reduce-scatter.48
  777.1 62.0 all-gather.37
  840.9 61.9 all-gather.39
  1017.3 27.1 reduce-scatter.38
  1144.7 27.4 reduce-scatter.40
  1175.2 80.7 reduce-scatter.42
  1320.5 55.4 reduce-scatter.54
  1378.4 59.2 reduce-scatter.46
  1439.9 59.1 reduce-scatter.44
Sparse Core Ops, SparseCore 1:
  237.8 36.5 all-gather.31
  301.8 31.1 all-gather.23
  334.6 77.5 all-gather.29
  432.5 77.8 all-gather.35
  512.2 63.8 all-gather.33
  590.2 27.5 reduce-scatter.34
  658.4 31.3 all-gather.25
  704.6 61.3 reduce-scatter.52
  918.0 22.9 reduce-scatter.36
  982.5 31.3 all-gather.27
  1052.6 82.2 all-reduce.20
where the time goes:
time: 1550 us; the launch traced here: 1540 us
  waiting for transfers between devices  741 us (48%)
  blocking collectives  483 us (31%)
  local copies, waits for them, and re-layouts  107 us (7%)
  matrix products  98.2 us (6%)
  other arithmetic  58.9 us (4%)
  starting transfers between devices  33.8 us (2%)
  between operations  18.8 us (1%)
    psum x8, blocking collectives, width_total(): return lax.psum(values, ('row', 'col'))  145 us
    unnamed x35, waiting for transfers between devices  141 us
    unnamed x2, blocking collectives  123 us
    all_gather x4, waiting for transfers between devices, spread_width(): return lax.all_gather(values, 'col', axis=1, tiled=True)  89.1 us
    unnamed x181, local copies, waits for them, and re-layouts  66.2 us
    all_gather x1, waiting for transfers between devices, on_device(): lax.all_gather(w_gate, 'dp', axis=1, tiled=True)  64.2 us
    psum x1, waiting for transfers between devices, on_device(): lax.psum(key_partial.astype(jnp.bfloat16), ('row', 'col'))  63.5 us
    all_gather x1, waiting for transfers between devices, on_device(): lax.all_gather(activated.astype(jnp.bfloat16), 'row', axis=1, tiled=True)  61.5 us
  transfers between devices with their start and end apart: 34, of which 19 were waited for; matrix products, arithmetic and copies ran while one was open for 16% of the time, Pallas kernels for 0%

commit v1 on v0

v1 whole, which is shorter than its diff:
```python
import math

import jax
import jax.numpy as jnp
from jax import lax
from jax.experimental import pallas as pl
from jax.experimental.pallas import tpu as pltpu
from jax.sharding import Mesh, PartitionSpec as P

D = 1152
HALF = 576
H = 4
HD = 256
FF = 6912
LEN = 1216
OWN = 152
UNITS = 54
PADDED = 56
DOWN_A = 32
DOWN_B = PADDED - DOWN_A
EPSILON = 1e-06
ROPE_BASE = 1000000.0
MASKED = -1e30
SCALE = HD ** (-0.5)
Z = ("zl", "zh")
LOW = jnp.bfloat16
F32 = jnp.float32


def shift(v, axis, step):
    if axis == Z:
        own = [(i % 2) * 2 + i // 2 for i in range(4)]
        return lax.ppermute(v, axis, [(own[i], own[(i + step) % 4]) for i in range(4)])
    size = lax.axis_size(axis)
    return lax.ppermute(v, axis, [(i, (i + step) % size) for i in range(size)])


def swap(v, axis):
    return shift(v, axis, 1)


def gather_direct(v, axis):
    return [v, shift(v, axis, -1), shift(v, axis, -2), shift(v, axis, 1)]


def half_of(v):
    if v.ndim > 2:
        return v.shape[0] // 2
    return (v.shape[0] // 2 + 7) // 8 * 8


def gather_ring(v, axis):
    half = half_of(v)
    before = shift(v, axis, 1)
    after = shift(v, axis, -1)
    opposite = jnp.concatenate(
        [shift(before[:half], axis, 1), shift(after[half:], axis, -1)], axis=0
    )
    return [v, after, opposite, before]


def add(*parts):
    total = parts[0].astype(F32)
    for part in parts[1:]:
        total = total + part.astype(F32)
    return total


def scatter_ring(blocks, axis):
    own, after, opposite, before = blocks
    half = half_of(own)
    passed_up = shift(opposite[:half], axis, 1)
    passed_down = shift(opposite[half:], axis, -1)
    up = jnp.concatenate([add(after[:half], passed_up).astype(LOW), after[half:]], axis=0)
    down = jnp.concatenate([before[:half], add(before[half:], passed_down).astype(LOW)], axis=0)
    return add(own, shift(up, axis, 1), shift(down, axis, -1))


def scatter_direct(blocks, axis):
    own, after, opposite, before = blocks
    return add(own, shift(after, axis, 1), shift(opposite, axis, 2), shift(before, axis, -1))


def whole(shape, dtype):
    return jax.ShapeDtypeStruct(shape, dtype)


VMEM = pl.BlockSpec(memory_space=pltpu.VMEM)
SMEM = pl.BlockSpec(memory_space=pltpu.SMEM)
BIG = pltpu.CompilerParams(vmem_limit_bytes=32 * 1024 * 1024)


def row_blocks(place_ref):
    for y in range(4):
        for zl in range(2):
            first = place_ref[(y * 2 + zl) * 2]
            second = place_ref[(y * 2 + zl) * 2 + 1]
            for side in range(2):
                row = y * 64 + zl * 32 + place_ref[16 + side] * 16
                yield side, first, second, pl.multiple_of(row, 16)


def joined(ref, first, second):
    pair = [ref[first].astype(F32), ref[second].astype(F32)]
    return jnp.concatenate(pair, axis=0).astype(LOW)


def assemble_heads(place, mine, other):
    heads = mine.shape[0]

    def kernel(place_ref, mine_ref, other_ref, out_ref):
        for side, first, second, row in row_blocks(place_ref):
            ref = other_ref if side else mine_ref
            for h in range(heads):
                out_ref[pl.ds(row + h * HD, 16), :] = joined(ref.at[h], first, second)

    return pl.pallas_call(
        kernel,
        out_shape=whole((heads * HD, D), LOW),
        in_specs=[SMEM, VMEM, VMEM],
        out_specs=VMEM,
        compiler_params=BIG,
    )(place, mine, other)


def assemble_pair(place, mine, other):
    def kernel(place_ref, mine_ref, other_ref, key_ref, value_ref, gain_ref):
        for side, first, second, row in row_blocks(place_ref):
            ref = other_ref if side else mine_ref
            key_ref[pl.ds(row, 16), :] = joined(ref.at[0], first, second)
            value_ref[pl.ds(row, 16), :] = joined(ref.at[1], first, second)
        total = mine_ref[2, 0].astype(F32) + other_ref[2, 0].astype(F32)
        for k in range(1, 16):
            total = total + mine_ref[2, k].astype(F32) + other_ref[2, k].astype(F32)
        gain_ref[...] = total

    return pl.pallas_call(
        kernel,
        out_shape=(whole((HD, D), LOW), whole((HD, D), LOW), whole((8, D), F32)),
        in_specs=[SMEM, VMEM, VMEM],
        out_specs=(VMEM, VMEM, VMEM),
        compiler_params=BIG,
    )(place, mine, other)


def divide_heads(place, grad):
    heads = grad.shape[0] // HD

    def kernel(place_ref, grad_ref, mine_ref, other_ref):
        for side, first, second, row in row_blocks(place_ref):
            ref = other_ref if side else mine_ref
            for h in range(heads):
                rows = grad_ref[pl.ds(row + h * HD, 16), :].astype(F32)
                ref[h, first] = rows[:8].astype(LOW)
                ref[h, second] = rows[8:].astype(LOW)

    return pl.pallas_call(
        kernel,
        out_shape=(whole((heads, 16, 8, D), LOW),) * 2,
        in_specs=[SMEM, VMEM],
        out_specs=(VMEM, VMEM),
        compiler_params=BIG,
    )(place, grad)


def divide_pair(place, key_grad, value_grad, gain_grad):
    def kernel(place_ref, key_ref, value_ref, gain_ref, mine_ref, other_ref):
        gains = gain_ref[...].astype(LOW)
        for side, first, second, row in row_blocks(place_ref):
            ref = other_ref if side else mine_ref
            for part, grad_ref in enumerate((key_ref, value_ref)):
                rows = grad_ref[pl.ds(row, 16), :].astype(F32)
                ref[first, part] = rows[:8].astype(LOW)
                ref[second, part] = rows[8:].astype(LOW)
            ref[first, 2] = gains
            ref[second, 2] = gains

    return pl.pallas_call(
        kernel,
        out_shape=(whole((16, 3, 8, D), LOW),) * 2,
        in_specs=[SMEM, VMEM, VMEM, VMEM],
        out_specs=(VMEM, VMEM),
        compiler_params=BIG,
    )(place, key_grad, value_grad, gain_grad)


def dot_nt(a, b):
    return lax.dot_general(a, b, (((1,), (1,)), ((), ())), preferred_element_type=F32)


def dot_nn(a, b):
    return lax.dot_general(a, b, (((1,), (0,)), ((), ())), preferred_element_type=F32)


def dot_tn(a, b):
    return lax.dot_general(a, b, (((0,), (0,)), ((), ())), preferred_element_type=F32)


def inverse_rms(values):
    return lax.rsqrt(jnp.mean(values * values, axis=-1, keepdims=True) + EPSILON)


def norm_backward(upstream, source, inverse, gain_row):
    weighted = upstream * gain_row
    inner = jnp.mean(weighted * source, axis=-1, keepdims=True)
    source_grad = inverse * weighted - source * (inverse * inverse * inverse) * inner
    gain_grad = jnp.sum(upstream * source * inverse, axis=0)
    return source_grad, gain_grad


def rotary_tables(places):
    frequencies = jnp.exp(
        jnp.arange(HD // 2, dtype=F32) * (-2.0 * math.log(ROPE_BASE) / HD)
    )
    angles = places.astype(F32)[:, None] * frequencies[None, :]
    return jnp.cos(angles), jnp.sin(angles)


def rotate(values, cosine, sine):
    front, back = values[..., : HD // 2], values[..., HD // 2 :]
    return jnp.concatenate(
        [front * cosine - back * sine, back * cosine + front * sine], axis=-1
    )


def in_order(first, mine, other):
    return jnp.where(first, mine, other), jnp.where(first, other, mine)


def on_device(
    hidden_in,
    segments,
    positions,
    out_grad,
    w_query,
    w_key,
    w_value,
    w_out,
    w_gate,
    w_up,
    w_down,
    norm_gains,
    head_gains,
):
    iy = lax.axis_index("y")
    izh = lax.axis_index("zh")
    iz = izh * 2 + lax.axis_index("zl")
    ix = lax.axis_index("x")
    ic = lax.axis_index("core")
    izl = lax.axis_index("zl")
    ring = jnp.arange(4, dtype=jnp.int32)
    z_of = jnp.array([0, 2, 1, 3], jnp.int32)
    place = jnp.concatenate(
        [
            (((ring - iy) % 4)[:, None] * 4 + ((z_of - iz) % 4)[None, :]).reshape(16),
            jnp.stack([ic, 1 - ic]).astype(jnp.int32),
        ]
    )

    def whole_rows(turned):
        count = turned.shape[-2] // 2
        turned = turned.reshape(turned.shape[:-2] + (2, count, HALF))
        axis = turned.ndim - 3
        mine = lax.dynamic_index_in_dim(turned, izh, axis, False)
        other = swap(lax.dynamic_index_in_dim(turned, 1 - izh, axis, False), "zh")
        return jnp.concatenate(in_order(izh == 0, mine, other), axis=-1)

    def shard_rows(rows):
        turned = rows.reshape(rows.shape[:-1] + (2, HALF))
        axis = turned.ndim - 2
        mine = lax.dynamic_index_in_dim(turned, izh, axis, False)
        other = lax.dynamic_index_in_dim(turned, 1 - izh, axis, False).astype(LOW)
        other = swap(other, "zh").astype(F32)
        return jnp.concatenate(in_order(izh == 0, mine, other), axis=-2)

    gain_place = (((izh * 4 + ix) * 4 + iy) * 4 + izl * 2 + ic) * 9
    head_place = (iy * 4 + izl * 2 + ic) * 16
    gains = lax.dynamic_update_slice(jnp.zeros((4, D), LOW), norm_gains, (0, gain_place))
    heads = lax.dynamic_update_slice(jnp.zeros((2, HD), LOW), head_gains, (0, head_place))
    heads = jnp.where((izh == 0) & (ix == 0), heads, jnp.zeros((), LOW)).reshape(1, 2 * HD)
    misc = jnp.concatenate(
        [gains, jnp.pad(heads, ((0, 0), (0, D - 2 * HD))), jnp.zeros((3, D), LOW)], axis=0
    )
    misc = add(*gather_direct(misc, "x")).astype(LOW)
    rows = whole_rows(jnp.stack([w_key.T, w_value.T, w_query.T]))
    pack = jnp.concatenate([rows.reshape(24, D), misc], axis=0)
    pack = jnp.stack(gather_direct(pack, Z))
    pack = jnp.concatenate(gather_ring(pack, "y"), axis=0).reshape(16, 4, 8, D)
    pack = pack.transpose(1, 0, 2, 3)
    pair_part = jnp.stack([pack[0], pack[1], pack[3]])
    key_weight, value_weight, misc = assemble_pair(place, pair_part, swap(pair_part, "core"))
    gain_rows = misc[:4]
    head_gain = misc[4, : 2 * HD].reshape(2, HD)
    query_part = jnp.stack(gather_ring(pack[2], "x"))
    query_weight = assemble_heads(place, query_part, swap(query_part, "core"))

    stream = hidden_in.astype(F32)
    scale_one = inverse_rms(stream)
    normed_one = (stream * scale_one * gain_rows[0]).astype(LOW)
    key_raw = dot_nt(normed_one, key_weight)
    value_low = dot_nt(normed_one, value_weight).astype(LOW)
    token_start = (izh * 4 + ix) * OWN
    own_positions = lax.dynamic_slice_in_dim(positions, token_start, OWN)
    own_segments = lax.dynamic_slice_in_dim(segments, token_start, OWN)
    cosine, sine = rotary_tables(own_positions)
    key_rot, key_back = jax.vjp(
        lambda raw, gain: rotate(raw * inverse_rms(raw) * gain, cosine, sine),
        key_raw,
        head_gain[1],
    )
    pair = jnp.concatenate([key_rot.astype(LOW), value_low], axis=1)
    pair = jnp.stack([pair, swap(pair, "zh")])
    pair = jnp.concatenate(gather_ring(pair, "x"), axis=0)
    pair = pair.reshape(LEN, 2 * HD)
    keys, values = pair[:, :HD], pair[:, HD:]
    key_start = jnp.stack(
        [((izh + b) % 2 * 4 + (ix + a) % 4) * OWN for a in range(4) for b in range(2)]
    )
    key_order = (key_start[:, None] + jnp.arange(OWN, dtype=jnp.int32)[None, :]).reshape(LEN)
    key_segments = jnp.concatenate(
        [lax.dynamic_slice_in_dim(segments, key_start[k], OWN) for k in range(8)]
    )

    query_raw = dot_nt(normed_one, query_weight).reshape(OWN, H, HD)
    query_norm, query_back = jax.vjp(
        lambda raw, gain: rotate(
            raw * inverse_rms(raw) * gain, cosine[:, None, :], sine[:, None, :]
        ),
        query_raw,
        head_gain[0],
    )
    query_rot = query_norm.astype(LOW).transpose(1, 0, 2).reshape(H * OWN, HD)
    query_order = token_start + jnp.arange(OWN, dtype=jnp.int32)
    allowed = (own_segments[:, None] == key_segments[None, :]) & (
        query_order[:, None] >= key_order[None, :]
    )
    scores = (dot_nt(query_rot, keys) * SCALE).reshape(H, OWN, LEN)
    scores = jnp.where(allowed[None], scores, MASKED)
    exponent = jnp.exp(scores - jnp.max(scores, axis=-1, keepdims=True))
    probs = (exponent / jnp.sum(exponent, axis=-1, keepdims=True)).reshape(H * OWN, LEN)
    probs_low = probs.astype(LOW)
    context = dot_nn(probs_low, values).astype(LOW)
    context = context.reshape(H, OWN, HD).transpose(1, 0, 2).reshape(OWN, H * HD)

    across = ("y", "zl", "core", "zh")
    down_rows = jnp.concatenate(
        [w_down.reshape(32, UNITS, 36), w_out.reshape(32, 8, 36)], axis=1
    )
    down_rows = lax.all_to_all(down_rows, across, 0, 0, tiled=True)
    down_rows = (
        down_rows.reshape(16, 2, UNITS + 8, 36).transpose(2, 1, 0, 3).reshape(UNITS + 8, D)
    )

    def pad_units(v):
        return jnp.pad(v, ((0, PADDED - UNITS), (0, 0)))

    rows = whole_rows(jnp.stack([w_gate.T, w_up.T]))
    gate_rows, up_rows = pad_units(rows[0]), pad_units(rows[1])
    out_rows = down_rows[UNITS:]
    down_rows = pad_units(down_rows[:UNITS])
    side_a = jnp.concatenate([gate_rows, down_rows[:DOWN_A], out_rows], axis=0)
    side_b = jnp.concatenate([up_rows, down_rows[DOWN_A:]], axis=0)
    side_a = jnp.stack(gather_ring(jnp.stack(gather_ring(side_a, "y")), Z))
    side_b = jnp.stack(gather_ring(jnp.stack(gather_ring(side_b, Z)), "y"), axis=1)
    units = 16 * PADDED
    gate_weight = side_a[:, :, :PADDED].reshape(units, D)
    up_weight = side_b[:, :, :PADDED].reshape(units, D)
    down_weight = jnp.concatenate(
        [side_a[:, :, PADDED : PADDED + DOWN_A], side_b[:, :, PADDED:]], axis=2
    ).reshape(units, D)
    out_part = side_a[:, :, PADDED + DOWN_A :].transpose(1, 0, 2, 3).reshape(16, 8, D)
    out_part = jnp.stack(gather_ring(out_part, "x"))
    out_weight = assemble_heads(place, out_part, swap(out_part, "core"))

    def spread_tokens(v):
        mine = jnp.concatenate(gather_ring(v, "x"), axis=0)
        return jnp.concatenate([mine, swap(mine, "core")], axis=0)

    def sum_tokens(v):
        v = v.reshape(2, 4, OWN, D)
        mine = add(v[0], swap(v[1], "core")).astype(LOW)
        return scatter_ring([mine[0], mine[1], mine[2], mine[3]], "x")

    attn_raw = dot_nn(context, out_weight)
    scale_two = inverse_rms(attn_raw)
    middle = stream + attn_raw * scale_two * gain_rows[1]
    scale_three = inverse_rms(middle)
    normed_two = (middle * scale_three * gain_rows[2]).astype(LOW)
    wide_two = spread_tokens(normed_two)
    gate_raw = dot_nt(wide_two, gate_weight)
    up_raw = dot_nt(wide_two, up_weight)
    activated, gelu_back = jax.vjp(
        lambda gate, up: jax.nn.gelu(gate, approximate=True) * up, gate_raw, up_raw
    )
    hidden = activated.astype(LOW)
    down_raw = sum_tokens(dot_nn(hidden, down_weight).astype(LOW))
    scale_four = inverse_rms(down_raw)
    result = (middle + down_raw * scale_four * gain_rows[3]).astype(LOW)
    upstream = out_grad.astype(F32)
    down_grad, gain_four = norm_backward(upstream, down_raw, scale_four, gain_rows[3])
    down_wide = spread_tokens(down_grad.astype(LOW))
    hidden_grad = dot_nt(down_wide, down_weight)
    gate_grad, up_grad = gelu_back(hidden_grad)
    gate_low, up_low = gate_grad.astype(LOW), up_grad.astype(LOW)
    normed_two_grad = sum_tokens(
        (dot_nn(gate_low, gate_weight) + dot_nn(up_low, up_weight)).astype(LOW)
    )
    grad_down = dot_tn(hidden, down_wide).astype(LOW).reshape(4, 4, PADDED, D)
    grad_gate = dot_tn(gate_low, wide_two).astype(LOW).reshape(4, 4, PADDED, D)
    grad_up = dot_tn(up_low, wide_two).astype(LOW).reshape(4, 4, PADDED, D)
    side_a = jnp.concatenate([grad_gate, grad_down[:, :, :DOWN_A]], axis=2)
    side_b = jnp.concatenate([grad_up, grad_down[:, :, DOWN_A:]], axis=2)
    side_a = scatter_ring(list(side_a), Z).astype(LOW)
    side_a = scatter_ring(list(side_a), "y")
    side_b = scatter_ring([side_b[:, k] for k in range(4)], "y").astype(LOW)
    side_b = scatter_ring(list(side_b), Z)

    both = shard_rows(jnp.stack([side_a[:UNITS], side_b[:UNITS]]))
    gate_shard, up_shard = both[0].T, both[1].T
    down_rows = jnp.concatenate([side_a[PADDED:], side_b[PADDED:]], axis=0)[:UNITS].astype(LOW)

    middle_part, gain_three = norm_backward(normed_two_grad, middle, scale_three, gain_rows[2])
    middle_grad = upstream + middle_part
    attn_grad, gain_two = norm_backward(middle_grad, attn_raw, scale_two, gain_rows[1])
    attn_low = attn_grad.astype(LOW)
    context_grad = dot_nt(attn_low, out_weight).astype(LOW)
    context_grad = context_grad.reshape(OWN, H, HD).transpose(1, 0, 2).reshape(H * OWN, HD)
    prob_grad = dot_nt(context_grad, values)
    centre = jnp.sum(probs * prob_grad, axis=-1, keepdims=True)
    score_low = (probs * (prob_grad - centre)).astype(LOW)
    key_part = dot_tn(score_low, query_rot) * SCALE
    value_part = dot_tn(probs_low, context_grad)
    pair_grad = jnp.concatenate([key_part, value_part], axis=1).astype(LOW)
    pair_grad = pair_grad.reshape(4, 2, OWN, 2 * HD)
    pair_grad = scatter_ring(list(pair_grad), "x")
    pair_grad = add(pair_grad[0], swap(pair_grad[1].astype(LOW), "zh"))
    query_grad = (dot_nn(score_low, keys) * SCALE).reshape(H, OWN, HD).transpose(1, 0, 2)
    query_raw_grad, query_gain = query_back(query_grad)
    query_low = query_raw_grad.reshape(OWN, H * HD).astype(LOW)
    key_raw_grad, key_gain = key_back(pair_grad[:, :HD])
    key_low = key_raw_grad.astype(LOW)
    value_grad_low = pair_grad[:, HD:].astype(LOW)
    normed_one_grad = (
        dot_nn(query_low, query_weight)
        + dot_nn(key_low, key_weight)
        + dot_nn(value_grad_low, value_weight)
    )
    stream_part, gain_one = norm_backward(normed_one_grad, stream, scale_one, gain_rows[0])
    input_grad = (middle_grad + stream_part).astype(LOW)

    def over_groups(blocks):
        blocks = blocks.reshape((4, 4) + blocks.shape[1:])
        blocks = scatter_ring(list(blocks), "y").astype(LOW)
        return scatter_direct(list(blocks), Z)

    def over_heads(grad):
        mine, other = divide_heads(place, grad.astype(LOW))
        mine = add(mine, swap(other, "core")).astype(LOW)
        return over_groups(scatter_ring(list(mine), "x").astype(LOW))

    out_rows = over_heads(dot_tn(context, attn_low)).astype(LOW)
    down_rows = jnp.concatenate([down_rows, out_rows], axis=0)
    down_rows = down_rows.reshape(UNITS + 8, 2, 16, 36).transpose(2, 1, 0, 3)
    down_rows = lax.all_to_all(
        down_rows.reshape(32, UNITS + 8, 36), across, 0, 0, tiled=True
    ).astype(F32)
    down_shard = down_rows[:, :UNITS].reshape(32 * UNITS, 36)
    out_shard = down_rows[:, UNITS:].reshape(HD, 36)

    query_rows = over_heads(dot_tn(query_low, normed_one))
    gains_grad = jnp.stack([gain_one, gain_two, gain_three, gain_four])
    head_grad = jnp.concatenate([query_gain, key_gain]).reshape(1, 2 * HD)
    misc = jnp.concatenate(
        [gains_grad, jnp.pad(head_grad, ((0, 0), (0, D - 2 * HD))), jnp.zeros((3, D), F32)], axis=0
    )
    mine, other = divide_pair(
        place,
        dot_tn(key_low, normed_one).astype(LOW),
        dot_tn(value_grad_low, normed_one).astype(LOW),
        misc,
    )
    pair_rows = over_groups(add(mine, swap(other, "core")).astype(LOW)).astype(LOW)
    pair_rows = add(*gather_direct(pair_rows, "x"))
    rows = shard_rows(jnp.stack([query_rows, pair_rows[0], pair_rows[1]]))
    query_shard, key_shard, value_shard = rows[0].T, rows[1].T, rows[2].T
    gains_shard = lax.dynamic_slice(pair_rows[2], (0, gain_place), (4, 9))
    head_shard = lax.dynamic_slice(
        pair_rows[2, 4, : 2 * HD].reshape(2, HD), (0, head_place), (2, 16)
    )
    return (
        result,
        input_grad,
        query_shard,
        key_shard,
        value_shard,
        out_shard,
        gate_shard,
        up_shard,
        down_shard,
        gains_shard,
        head_shard,
    )


def solution(mesh):
    split = Mesh(mesh.devices.reshape(4, 2, 2, 2, 4), ("y", "zl", "core", "zh", "x"))
    dp = ("y", "zl", "core")
    weights = (
        P("zh", ("x",) + dp),
        P("zh", dp),
        P("zh", dp),
        P("x", ("zh",) + dp),
        P("zh", ("x",) + dp),
        P("zh", ("x",) + dp),
        P("x", ("zh",) + dp),
        P(None, ("zh", "x") + dp),
        P(None, dp),
    )
    tokens = P(dp + ("zh", "x"), None)
    return jax.shard_map(
        on_device,
        mesh=split,
        in_specs=(tokens, P(dp), P(dp), tokens) + weights,
        out_specs=(tokens, tokens) + weights,
        check_vma=False,
    )
```

time: 1550 us -> 530 us (0.34)
  waiting for transfers between devices: 741 us -> 156 us
  blocking collectives: 483 us -> 0 us
  starting transfers between devices: 33.8 us -> 203 us
  local copies, waits for them, and re-layouts: 107 us -> 50.9 us
  matrix products: 98.2 us -> 52.9 us
    all_gather x10 -> x0, waiting for transfers between devices: 332 us -> none  [the longest x4 89.1 us: spread_width(): return lax.all_gather(values, 'col', axis=1, tiled=True)]
    psum x10 -> x0, blocking collectives: 207 us -> none  [the longest x8 145 us: width_total(): return lax.psum(values, ('row', 'col'))]
    reduce_scatter x9 -> x0, waiting for transfers between devices: 204 us -> none  [the longest x1 60.4 us: on_device(): lax.psum_scatter(grad_value_w.astype(jnp.bfloat16), 'dp', scatter_dimensi...]
    ppermute x0 -> x122, starting transfers between devices: none -> 178 us  [the longest x94 148 us: shift(): return lax.ppermute(v, axis, [(i, (i + step) % size) for i in range(size)])]
    ppermute x0 -> x122, waiting for transfers between devices: none -> 151 us  [the longest x94 118 us: shift(): return lax.ppermute(v, axis, [(i, (i + step) % size) for i in range(size)])]
    unnamed x35 -> x0, waiting for transfers between devices: 141 us -> none
    all_gather x8 -> x0, blocking collectives: 137 us -> none  [the longest x2 24.6 us: query_spread(): return lax.all_gather(values, 'row', axis=0, tiled=True)]
    unnamed x2 -> x0, blocking collectives: 123 us -> none
  transfers between devices with their start and end apart: 34 -> 124, of which waited for: 19 -> 49; matrix products, arithmetic and copies ran while one was open for 16% -> 17% of each run, Pallas kernels for 0% -> 1%
where the time goes in v1:
time: 530 us; the launch traced here: 520 us
  starting transfers between devices  203 us (38%)
  waiting for transfers between devices  156 us (29%)
  matrix products  52.9 us (10%)
  local copies, waits for them, and re-layouts  50.9 us (10%)
  other arithmetic  47.4 us (9%)
  Pallas kernels  6.45 us (1%)
    ppermute x94, starting transfers between devices, shift(): return lax.ppermute(v, axis, [(i, (i + step) % size) for i in range(size)])  148 us
    ppermute x94, waiting for transfers between devices, shift(): return lax.ppermute(v, axis, [(i, (i + step) % size) for i in range(size)])  118 us
    ppermute x28, waiting for transfers between devices, shift(): lax.ppermute(v, axis, [(own[i], own[(i + step) % 4]) for i in range(4)])  33.3 us
    ppermute x28, starting transfers between devices, shift(): lax.ppermute(v, axis, [(own[i], own[(i + step) % 4]) for i in range(4)])  30 us
    dot_general x9, matrix products, dot_nt(): lax.dot_general(a, b, (((1,), (1,)), ((), ())), preferred_element_type=F32)  21.6 us
    all_to_all x1, starting transfers between devices, on_device(): lax.all_to_all(down_rows.reshape(32, UNITS + 8, 36), across, 0, 0, tiled=...  17.7 us
    dot_general x9, matrix products, dot_tn(): lax.dot_general(a, b, (((0,), (0,)), ((), ())), preferred_element_type=F32)  16.1 us
    dot_general x9, matrix products, dot_nn(): lax.dot_general(a, b, (((1,), (0,)), ((), ())), preferred_element_type=F32)  15.2 us
  transfers between devices with their start and end apart: 124, of which 49 were waited for; matrix products, arithmetic and copies ran while one was open for 17% of the time, Pallas kernels for 1%

profile of v1, /device:TPU:1, one launch (start us, length us, event | category | flops | bytes accessed | tf_op | source)
XLA Modules:
  0.0 520.4 jit_solution(726130521714118346)
XLA Ops:
  8.5 3.7 collective-permute-start
  17.0 6.9 %all-to-all-start = ((bf16[32,2,1116]{2,1,0:T(2,128)(2,1)}), bf16[32,2,1116]{2,1,0:T(2,128)(2,1)S(1)}, u32[]{:S(2)}, u32[]{:S(2)}) async-start(bf16[32,2,1116]{2,1,0:T(2,128)(2,1)} %reshape.660), calls=%async_computation | async-start | bytes 294912 | tf_op jit(solution)/shard_map/all_to_all | solution.py:349
  52.8 4.3 collective-permute-done.42
  73.6 7.7 %collective-permute-start.11 = (bf16[3,16,8,1152]{3,2,1,0:T(8,128)(2,1)S(1)}, bf16[3,16,8,1152]{3,2,1,0:T(8,128)(2,1)S(1)}, u32[]{:S(2)}, u32[]{:S(2)}) collective-permute-start(bf16[3,16,8,1152]{3,2,1,0:T(8,128)(2,1)S(1)} %pad_maximum_fusion.4.mine_ref), channel_id=1, source_target_pairs={{0,8},{8,0},{1,9},{9,1},{2,10},{10,2},{3,11},{11,3},{4,12},{12,4},... | collective-permute-start | bytes 2654216 | tf_op jit(solution)/shard_map/ppermute | solution.py:35
  89.8 10.2 %collective-permute-done.45 = bf16[4,80,1152]{2,1,0:T(8,128)(2,1)S(1)} collective-permute-done((bf16[4,80,1152]{2,1,0:T(8,128)(2,1)S(1)}, bf16[4,80,1152]{2,1,0:T(8,128)(2,1)S(1)}, u32[]{:S(2)}, u32[]{:S(2)}) %collective-permute-start.45) | collective-permute-done | bytes 737312 | tf_op jit(solution)/shard_map/ppermute | solution.py:35
  99.9 6.0 %collective-permute-start.16 = (bf16[4,16,8,1152]{3,2,1,0:T(8,128)(2,1)S(1)}, bf16[4,16,8,1152]{3,2,1,0:T(8,128)(2,1)S(1)}, u32[]{:S(2)}, u32[]{:S(2)}) collective-permute-start(bf16[4,16,8,1152]{3,2,1,0:T(8,128)(2,1)S(1)} %pad_maximum_fusion.2.mine_ref), channel_id=1, source_target_pairs={{0,8},{8,0},{1,9},{9,1},{2,10},{10,2},{3,11},{11,3},{4,12},{12,4},... | collective-permute-start | bytes 3538952 | tf_op jit(solution)/shard_map/ppermute | solution.py:35
  127.5 8.3 %collective-permute-done.19 = bf16[2,152,512]{2,1,0:T(8,128)(2,1)S(1)} collective-permute-done((bf16[2,152,512]{2,1,0:T(8,128)(2,1)S(1)}, bf16[2,152,512]{2,1,0:T(8,128)(2,1)S(1)}, u32[]{:S(2)}, u32[]{:S(2)}) %collective-permute-start.19) | collective-permute-done | bytes 311328 | tf_op jit(solution)/shard_map/ppermute | solution.py:35
  141.2 4.6 collective-permute-done.21
  162.6 3.9 collective-permute-start.35
  176.6 9.8 %collective-permute-done.37 = bf16[152,1152]{1,0:T(8,128)(2,1)S(1)} collective-permute-done((bf16[152,1152]{1,0:T(8,128)(2,1)S(1)}, bf16[152,1152]{1,0:T(8,128)(2,1)S(1)}, u32[]{:S(2)}, u32[]{:S(2)}) %collective-permute-start.37) | collective-permute-done | bytes 350240 | tf_op jit(solution)/shard_map/ppermute | solution.py:35
  201.6 5.5 %multiply_convert_fusion.1 = (bf16[1216,896]{1,0:T(8,128)(2,1)S(1)}, f32[1216,896]{1,0:T(8,128)}) fusion(f32[1216,896]{1,0:T(8,128)S(1)} %fusion.202, bf16[1216,1152]{1,0:T(8,128)(2,1)S(1)} %constant_dynamic-update-slice_fusion.17, bf16[896,1152]{1,0:T(8,128)(2,1)S(1)} %bitcast.571), kind=kOutput, calls=%fused_computation.25 | convolution fusion | flops 2521186304 | bytes 15761408 | tf_op jit(solution)/shard_map/dot_general | solution.py:188
  224.0 6.1 %collective-permute-done.53 = bf16[152,1152]{1,0:T(8,128)(2,1)S(1)} collective-permute-done((bf16[152,1152]{1,0:T(8,128)(2,1)S(1)}, bf16[152,1152]{1,0:T(8,128)(2,1)S(1)}, u32[]{:S(2)}, u32[]{:S(2)}) %collective-permute-start.53) | collective-permute-done | bytes 350240 | tf_op jit(solution)/shard_map/ppermute | solution.py:35
  237.9 5.7 %collective-permute-done.55 = bf16[152,1152]{1,0:T(8,128)(2,1)S(1)} collective-permute-done((bf16[152,1152]{1,0:T(8,128)(2,1)S(1)}, bf16[152,1152]{1,0:T(8,128)(2,1)S(1)}, u32[]{:S(2)}, u32[]{:S(2)}) %collective-permute-start.55) | collective-permute-done | bytes 350240 | tf_op jit(solution)/shard_map/ppermute | solution.py:35
  249.5 4.6 collective-permute-start.58
  260.3 8.3 %multiply_convert_fusion = (bf16[1216,896]{1,0:T(8,128)(2,1)S(1)}, bf16[1216,896]{1,0:T(8,128)(2,1)S(1)}) fusion(f32[1216,896]{1,0:T(8,128)S(1)} %fusion.202, f32[1216,896]{1,0:T(8,128)} %get-tuple-element.282, bf16[1216,1152]{1,0:T(8,128)(2,1)S(1)} %constant_dynamic-update-slice_fusion.28, bf16[896,1152]{1,0:T(8,128)(2,1)S(1)} %bitcast.576), kind=kOutput, calls=%fused_computation.24 | convolution fusion | flops 2536439808 | bytes 17940480 | tf_op jit(solution)/shard_map/dot_general | solution.py:188
  278.5 3.8 fusion
  296.4 4.1 collective-permute-done.93
  303.2 7.5 %collective-permute-done.104 = bf16[4,80,1152]{2,1,0:T(8,128)(2,1)S(1)} collective-permute-done((bf16[4,80,1152]{2,1,0:T(8,128)(2,1)S(1)}, bf16[4,80,1152]{2,1,0:T(8,128)(2,1)S(1)}, u32[]{:S(2)}, u32[]{:S(2)}) %collective-permute-start.104) | collective-permute-done | bytes 737312 | tf_op jit(solution)/shard_map/ppermute | solution.py:35
  325.1 11.4 %collective-permute-done.94 = bf16[4,88,1152]{2,1,0:T(8,128)(2,1)S(1)} collective-permute-done((bf16[4,88,1152]{2,1,0:T(8,128)(2,1)S(1)}, bf16[4,88,1152]{2,1,0:T(8,128)(2,1)S(1)}, u32[]{:S(2)}, u32[]{:S(2)}) %collective-permute-start.94) | collective-permute-done | bytes 811040 | tf_op jit(solution)/shard_map/ppermute | solution.py:33
  373.0 4.6 collective-permute-done.61
  401.0 11.3 %collective-permute-start.69 = (bf16[4,16,8,1152]{3,2,1,0:T(8,128)(2,1)}, bf16[4,16,8,1152]{3,2,1,0:T(8,128)(2,1)}, u32[]{:S(2)}, u32[]{:S(2)}) collective-permute-start(bf16[4,16,8,1152]{3,2,1,0:T(8,128)(2,1)} %get-tuple-element.24), channel_id=1, source_target_pairs={{0,8},{8,0},{1,9},{9,1},{2,10},{10,2},{3,11},{11,3},{4,12},{12,4},... | collective-permute-start | bytes 3538952 | tf_op jit(solution)/shard_map/ppermute | solution.py:35
  419.6 4.5 collective-permute-start.109
  486.6 17.7 %all-to-all-start.1 = ((bf16[32,2,1116]{2,1,0:T(2,128)(2,1)}), bf16[32,2,1116]{2,1,0:T(2,128)(2,1)S(1)}, u32[]{:S(2)}, u32[]{:S(2)}) async-start(bf16[32,2,1116]{2,1,0:T(2,128)(2,1)} %reshape.662), calls=%async_computation.1 | async-start | bytes 294912 | tf_op jit(solution)/shard_map/all_to_all | solution.py:464
  507.1 5.0 all-to-all-done.1
  (748 shorter events, 351.0 us)
Async XLA Ops:
  2.7 26.8 %collective-permute-start.3 = (bf16[8,1152]{1,0:T(8,128)(2,1)S(1)}, bf16[8,1152]{1,0:T(8,128)(2,1)S(1)}, u32[]{:S(2)}, u32[]{:S(2)}) collective-permute-start(bf16[8,1152]{1,0:T(8,128)(2,1)S(1)} %fusion.171), channel_id=1, source_target_pairs={{0,1},{1,2},{2,3},{3,0},{4,5},{5,6},{6,7},{7,4},{8,9},{9,10},{10,1... | collective-permute-start | bytes 55304 | tf_op jit(solution)/shard_map/ppermute | solution.py:35
  4.1 25.4 %collective-permute-start.2 = (bf16[8,1152]{1,0:T(8,128)(2,1)S(1)}, bf16[8,1152]{1,0:T(8,128)(2,1)S(1)}, u32[]{:S(2)}, u32[]{:S(2)}) collective-permute-start(bf16[8,1152]{1,0:T(8,128)(2,1)S(1)} %fusion.171), channel_id=1, source_target_pairs={{0,2},{1,3},{2,0},{3,1},{4,6},{5,7},{6,4},{7,5},{8,10},{9,11},{10,... | collective-permute-start | bytes 55304 | tf_op jit(solution)/shard_map/ppermute | solution.py:35
  6.6 23.0 %collective-permute-start.1 = (bf16[8,1152]{1,0:T(8,128)(2,1)S(1)}, bf16[8,1152]{1,0:T(8,128)(2,1)S(1)}, u32[]{:S(2)}, u32[]{:S(2)}) collective-permute-start(bf16[8,1152]{1,0:T(8,128)(2,1)S(1)} %fusion.171), channel_id=1, source_target_pairs={{0,3},{1,0},{2,1},{3,2},{4,7},{5,4},{6,5},{7,6},{8,11},{9,8},{10,9... | collective-permute-start | bytes 55304 | tf_op jit(solution)/shard_map/ppermute | solution.py:35
  8.5 21.1 %collective-permute-start = (bf16[3,8,576]{2,1,0:T(8,128)(2,1)S(1)}, bf16[3,8,576]{2,1,0:T(8,128)(2,1)S(1)}, u32[]{:S(2)}, u32[]{:S(2)}) collective-permute-start(bf16[3,8,576]{2,1,0:T(8,128)(2,1)S(1)} %dynamic-slice_bitcast_fusion.1), channel_id=1, source_target_pairs={{0,4},{4,0},{1,5},{5,1},{2,6},{6,2},{3,7},{7,3},{8,12},{12,8},{9,1... | collective-permute-start | bytes 82952 | tf_op jit(solution)/shard_map/ppermute | solution.py:35
  17.0 24.7 %all-to-all-start = ((bf16[32,2,1116]{2,1,0:T(2,128)(2,1)}), bf16[32,2,1116]{2,1,0:T(2,128)(2,1)S(1)}, u32[]{:S(2)}, u32[]{:S(2)}) async-start(bf16[32,2,1116]{2,1,0:T(2,128)(2,1)} %reshape.660), calls=%async_computation | async-start | bytes 294912 | tf_op jit(solution)/shard_map/all_to_all | solution.py:349
  38.3 22.9 %collective-permute-start.7 = (bf16[4,32,1152]{2,1,0:T(8,128)(2,1)}, bf16[4,32,1152]{2,1,0:T(8,128)(2,1)S(1)}, u32[]{:S(2)}, u32[]{:S(2)}) collective-permute-start(bf16[4,32,1152]{2,1,0:T(8,128)(2,1)} %pad_maximum_fusion.21), channel_id=1, source_target_pairs={{0,96},{32,0},{64,32},{96,64},{1,97},{33,1},{65,33},{97,65},{2,98}... | collective-permute-start | bytes 884744 | tf_op jit(solution)/shard_map/ppermute | solution.py:35
  40.8 20.3 %collective-permute-start.8 = (bf16[4,32,1152]{2,1,0:T(8,128)(2,1)}, bf16[4,32,1152]{2,1,0:T(8,128)(2,1)S(1)}, u32[]{:S(2)}, u32[]{:S(2)}) collective-permute-start(bf16[4,32,1152]{2,1,0:T(8,128)(2,1)} %pad_maximum_fusion.21), channel_id=1, source_target_pairs={{0,32},{32,64},{64,96},{96,0},{1,33},{33,65},{65,97},{97,1},{2,34}... | collective-permute-start | bytes 884744 | tf_op jit(solution)/shard_map/ppermute | solution.py:35
  70.7 38.7 %collective-permute-start.28 = (bf16[4,96,1152]{2,1,0:T(8,128)(2,1)S(1)}, bf16[4,96,1152]{2,1,0:T(8,128)(2,1)S(1)}, u32[]{:S(2)}, u32[]{:S(2)}) collective-permute-start(bf16[4,96,1152]{2,1,0:T(8,128)(2,1)S(1)} %get-tuple-element.173), channel_id=1, source_target_pairs={{0,16},{16,4},{4,20},{20,0},{1,17},{17,5},{5,21},{21,1},{2,18},{18... | collective-permute-start | bytes 2654216 | tf_op jit(solution)/shard_map/ppermute | solution.py:33
  70.8 38.4 %collective-permute-start.27 = (bf16[4,96,1152]{2,1,0:T(8,128)(2,1)S(1)}, bf16[4,96,1152]{2,1,0:T(8,128)(2,1)S(1)}, u32[]{:S(2)}, u32[]{:S(2)}) collective-permute-start(bf16[4,96,1152]{2,1,0:T(8,128)(2,1)S(1)} %get-tuple-element.173), channel_id=1, source_target_pairs={{0,20},{16,0},{4,16},{20,4},{1,21},{17,1},{5,17},{21,5},{2,22},{18... | collective-permute-start | bytes 2654216 | tf_op jit(solution)/shard_map/ppermute | solution.py:33
  73.6 37.1 %collective-permute-start.11 = (bf16[3,16,8,1152]{3,2,1,0:T(8,128)(2,1)S(1)}, bf16[3,16,8,1152]{3,2,1,0:T(8,128)(2,1)S(1)}, u32[]{:S(2)}, u32[]{:S(2)}) collective-permute-start(bf16[3,16,8,1152]{3,2,1,0:T(8,128)(2,1)S(1)} %pad_maximum_fusion.4.mine_ref), channel_id=1, source_target_pairs={{0,8},{8,0},{1,9},{9,1},{2,10},{10,2},{3,11},{11,3},{4,12},{12,4},... | collective-permute-start | bytes 2654216 | tf_op jit(solution)/shard_map/ppermute | solution.py:35
  86.3 19.7 %collective-permute-start.46 = (bf16[4,80,1152]{2,1,0:T(8,128)(2,1)S(1)}, bf16[4,80,1152]{2,1,0:T(8,128)(2,1)S(1)}, u32[]{:S(2)}, u32[]{:S(2)}) collective-permute-start(bf16[4,80,1152]{2,1,0:T(8,128)(2,1)S(1)} %get-tuple-element.189), channel_id=1, source_target_pairs={{0,32},{32,64},{64,96},{96,0},{1,33},{33,65},{65,97},{97,1},{2,34}... | collective-permute-start | bytes 2211848 | tf_op jit(solution)/shard_map/ppermute | solution.py:35
  99.9 50.9 %collective-permute-start.16 = (bf16[4,16,8,1152]{3,2,1,0:T(8,128)(2,1)S(1)}, bf16[4,16,8,1152]{3,2,1,0:T(8,128)(2,1)S(1)}, u32[]{:S(2)}, u32[]{:S(2)}) collective-permute-start(bf16[4,16,8,1152]{3,2,1,0:T(8,128)(2,1)S(1)} %pad_maximum_fusion.2.mine_ref), channel_id=1, source_target_pairs={{0,8},{8,0},{1,9},{9,1},{2,10},{10,2},{3,11},{11,3},{4,12},{12,4},... | collective-permute-start | bytes 3538952 | tf_op jit(solution)/shard_map/ppermute | solution.py:35
  287.1 59.9 %collective-permute-start.59 = (bf16[4,152,1152]{2,1,0:T(8,128)(2,1)}, bf16[4,152,1152]{2,1,0:T(8,128)(2,1)}, u32[]{:S(2)}, u32[]{:S(2)}) collective-permute-start(bf16[4,152,1152]{2,1,0:T(8,128)(2,1)} %bitcast.97), channel_id=1, source_target_pairs={{0,8},{8,0},{1,9},{9,1},{2,10},{10,2},{3,11},{11,3},{4,12},{12,4},... | collective-permute-start | bytes 4202504 | tf_op jit(solution)/shard_map/ppermute | solution.py:35
  300.8 24.3 %collective-permute-start.96 = (bf16[4,88,1152]{2,1,0:T(8,128)(2,1)S(1)}, bf16[4,88,1152]{2,1,0:T(8,128)(2,1)S(1)}, u32[]{:S(2)}, u32[]{:S(2)}) collective-permute-start(bf16[4,88,1152]{2,1,0:T(8,128)(2,1)S(1)} %pad_maximum_fusion.7), channel_id=1, source_target_pairs={{0,20},{16,0},{4,16},{20,4},{1,21},{17,1},{5,17},{21,5},{2,22},{18... | collective-permute-start | bytes 2433032 | tf_op jit(solution)/shard_map/ppermute | solution.py:33
  317.0 19.5 %collective-permute-start.94 = (bf16[4,88,1152]{2,1,0:T(8,128)(2,1)S(1)}, bf16[4,88,1152]{2,1,0:T(8,128)(2,1)S(1)}, u32[]{:S(2)}, u32[]{:S(2)}) collective-permute-start(bf16[4,88,1152]{2,1,0:T(8,128)(2,1)S(1)} %pad_maximum_fusion.6), channel_id=1, source_target_pairs={{0,16},{16,4},{4,20},{20,0},{1,17},{17,5},{5,21},{21,1},{2,18},{18... | collective-permute-start | bytes 2433032 | tf_op jit(solution)/shard_map/ppermute | solution.py:33
  321.7 22.0 %collective-permute-start.108 = (bf16[80,1152]{1,0:T(8,128)(2,1)S(1)}, bf16[80,1152]{1,0:T(8,128)(2,1)S(1)}, u32[]{:S(2)}, u32[]{:S(2)}) collective-permute-start(bf16[80,1152]{1,0:T(8,128)(2,1)S(1)} %pad_maximum_fusion.33), channel_id=1, source_target_pairs={{0,20},{16,0},{4,16},{20,4},{1,21},{17,1},{5,17},{21,5},{2,22},{18... | collective-permute-start | bytes 552968 | tf_op jit(solution)/shard_map/ppermute | solution.py:33
  401.0 33.6 %collective-permute-start.69 = (bf16[4,16,8,1152]{3,2,1,0:T(8,128)(2,1)}, bf16[4,16,8,1152]{3,2,1,0:T(8,128)(2,1)}, u32[]{:S(2)}, u32[]{:S(2)}) collective-permute-start(bf16[4,16,8,1152]{3,2,1,0:T(8,128)(2,1)} %get-tuple-element.24), channel_id=1, source_target_pairs={{0,8},{8,0},{1,9},{9,1},{2,10},{10,2},{3,11},{11,3},{4,12},{12,4},... | collective-permute-start | bytes 3538952 | tf_op jit(solution)/shard_map/ppermute | solution.py:35
  419.6 19.5 %collective-permute-start.109 = (bf16[4,16,8,1152]{3,2,1,0:T(8,128)(2,1)}, bf16[4,16,8,1152]{3,2,1,0:T(8,128)(2,1)}, u32[]{:S(2)}, u32[]{:S(2)}) collective-permute-start(bf16[4,16,8,1152]{3,2,1,0:T(8,128)(2,1)} %get-tuple-element.28), channel_id=1, source_target_pairs={{0,8},{8,0},{1,9},{9,1},{2,10},{10,2},{3,11},{11,3},{4,12},{12,4},... | collective-permute-start | bytes 3538952 | tf_op jit(solution)/shard_map/ppermute | solution.py:35
  454.4 28.4 %collective-permute-start.85 = (bf16[4,3,8,1152]{3,2,1,0:T(8,128)(2,1)S(1)}, bf16[4,3,8,1152]{3,2,1,0:T(8,128)(2,1)S(1)}, u32[]{:S(2)}, u32[]{:S(2)}) collective-permute-start(bf16[4,3,8,1152]{3,2,1,0:T(8,128)(2,1)S(1)} %pad_maximum_fusion.29), channel_id=1, source_target_pairs={{0,96},{32,0},{64,32},{96,64},{1,97},{33,1},{65,33},{97,65},{2,98}... | collective-permute-start | bytes 663560 | tf_op jit(solution)/shard_map/ppermute | solution.py:35
  457.2 25.6 %collective-permute-start.83 = (bf16[4,3,8,1152]{3,2,1,0:T(8,128)(2,1)S(1)}, bf16[4,3,8,1152]{3,2,1,0:T(8,128)(2,1)S(1)}, u32[]{:S(2)}, u32[]{:S(2)}) collective-permute-start(bf16[4,3,8,1152]{3,2,1,0:T(8,128)(2,1)S(1)} %pad_maximum_fusion.28), channel_id=1, source_target_pairs={{0,32},{32,64},{64,96},{96,0},{1,33},{33,65},{65,97},{97,1},{2,34}... | collective-permute-start | bytes 663560 | tf_op jit(solution)/shard_map/ppermute | solution.py:35
  482.9 21.4 %collective-permute-start.88 = (bf16[3,8,1152]{2,1,0:T(8,128)(2,1)S(1)}, bf16[3,8,1152]{2,1,0:T(8,128)(2,1)S(1)}, u32[]{:S(2)}, u32[]{:S(2)}) collective-permute-start(bf16[3,8,1152]{2,1,0:T(8,128)(2,1)S(1)} %get-tuple-element.221), channel_id=1, source_target_pairs={{0,20},{16,0},{4,16},{20,4},{1,21},{17,1},{5,17},{21,5},{2,22},{18... | collective-permute-start | bytes 165896 | tf_op jit(solution)/shard_map/ppermute | solution.py:33
  483.0 21.3 %collective-permute-start.87 = (bf16[3,8,1152]{2,1,0:T(8,128)(2,1)S(1)}, bf16[3,8,1152]{2,1,0:T(8,128)(2,1)S(1)}, u32[]{:S(2)}, u32[]{:S(2)}) collective-permute-start(bf16[3,8,1152]{2,1,0:T(8,128)(2,1)S(1)} %get-tuple-element.222), channel_id=1, source_target_pairs={{0,4},{16,20},{4,0},{20,16},{1,5},{17,21},{5,1},{21,17},{2,6},{18,... | collective-permute-start | bytes 165896 | tf_op jit(solution)/shard_map/ppermute | solution.py:33
  483.5 20.8 %collective-permute-start.86 = (bf16[3,8,1152]{2,1,0:T(8,128)(2,1)S(1)}, bf16[3,8,1152]{2,1,0:T(8,128)(2,1)S(1)}, u32[]{:S(2)}, u32[]{:S(2)}) collective-permute-start(bf16[3,8,1152]{2,1,0:T(8,128)(2,1)S(1)} %get-tuple-element.220), channel_id=1, source_target_pairs={{0,16},{16,4},{4,20},{20,0},{1,17},{17,5},{5,21},{21,1},{2,18},{18... | collective-permute-start | bytes 165896 | tf_op jit(solution)/shard_map/ppermute | solution.py:33
  486.6 25.5 %all-to-all-start.1 = ((bf16[32,2,1116]{2,1,0:T(2,128)(2,1)}), bf16[32,2,1116]{2,1,0:T(2,128)(2,1)S(1)}, u32[]{:S(2)}, u32[]{:S(2)}) async-start(bf16[32,2,1116]{2,1,0:T(2,128)(2,1)} %reshape.662), calls=%async_computation.1 | async-start | bytes 294912 | tf_op jit(solution)/shard_map/all_to_all | solution.py:464
  (198 other events, 1884.4 us)
